TPU v7x, 512 devices: a whole 4x8x8 slice. The times are simulated.
512 devices in a mesh: section: 16 (over z, core), tensor: 32 (over y, x).
Axes of the slice: x: 4, y: 8, z: 8, core: 2. Of those that a mesh axis runs over, the one named last changes fastest.
Arguments:
- resid: bfloat16 [128, 3584], P('tensor'), may hold values from -6 to 6
- w_enc: bfloat16 [114688, 3584], P(('section', 'tensor')), may hold values from -0.09375 to 0.09375
- b_enc: float32 [114688], P(('section', 'tensor')), may hold values from -1 to 0.5
- w_dec: bfloat16 [114688, 3584], P(('section', 'tensor')), may hold values from -0.015625 to 0.015625
- b_dec: float32 [3584], replicated, may hold values from -3 to 3
Outputs:
- recon: float32 [128, 3584], P('tensor')
- grad_w_dec: bfloat16 [114688, 3584], P(('section', 'tensor'))
- code_grad: float32 [128, 114688], P(None, ('section', 'tensor'))
- grad_b_dec: float32 [3584], replicated
- loss_value: float32 [], replicated
All inputs are finite; a program needn't handle non-finite values.
Results may differ from a plain program's by a relative error of at most 0.0032.
The roundings to bfloat16 on the way count: a program that leaves them out, or rounds other values in their place, can miss the bound.
Values may be sent and summed in bfloat16 or wider, within the bound.
A program may use at most 64 MiB of HBM per device.

v0:
```python
import jax
import jax.numpy as jnp
from jax import lax
from jax.sharding import PartitionSpec as P

epsilon = 1e-06


def per_device(resid, w_enc, b_enc, w_dec, b_dec):
    stream = lax.all_gather(resid, "tensor", axis=0, tiled=True)
    preact = (
        lax.dot_general(stream, w_enc, (((1,), (1,)), ((), ())), preferred_element_type=jnp.float32)
        + b_enc
    )
    codes = jnp.maximum(preact, 0.0).astype(jnp.bfloat16)
    codes_f32 = codes.astype(jnp.float32)
    dec_f32 = w_dec.astype(jnp.float32)
    dec_norm = jnp.sqrt(jnp.sum(dec_f32 * dec_f32, axis=1) + epsilon)
    penalty = lax.psum(jnp.sum(codes_f32 * dec_norm), ("section", "tensor"))
    own_rows = resid.shape[0]
    total_rows = stream.shape[0]
    model_width = stream.shape[1]
    partial_value = jnp.dot(codes, w_dec, preferred_element_type=jnp.float32)
    summed = lax.psum(partial_value, ("section", "tensor"))
    recon_all = summed + b_dec
    errors = recon_all - stream.astype(jnp.float32)
    first_row = lax.axis_index("tensor") * own_rows
    recon = lax.dynamic_slice_in_dim(recon_all, first_row, own_rows, 0)
    squares = jnp.sum(errors * errors)
    grad_b_dec = jnp.sum(errors, axis=0)
    err_half = errors.astype(jnp.bfloat16)
    loss_value = (0.5 * squares + penalty) / (total_rows * model_width)
    code_sums = jnp.sum(codes_f32, axis=0)
    grad_w_dec = lax.dot_general(
        codes, err_half, (((0,), (0,)), ((), ())), preferred_element_type=jnp.float32
    )
    grad_w_dec = grad_w_dec + code_sums[:, None] * dec_f32 / dec_norm[:, None]
    code_grad = (
        lax.dot_general(
            err_half, w_dec, (((1,), (1,)), ((), ())), preferred_element_type=jnp.float32
        )
        + dec_norm
    )
    return (recon, grad_w_dec.astype(jnp.bfloat16), code_grad, grad_b_dec, loss_value)


def solution(mesh):
    in_specs = (
        P("tensor", None),
        P(("section", "tensor"), None),
        P(("section", "tensor")),
        P(("section", "tensor"), None),
        P(),
    )
    out_specs = (
        P("tensor", None),
        P(("section", "tensor"), None),
        P(None, ("section", "tensor")),
        P(),
        P(),
    )
    return jax.shard_map(
        per_device, mesh=mesh, in_specs=in_specs, out_specs=out_specs, check_vma=False
    )
```

profile of v0, /device:TPU:1, one launch (start us, length us, event | category | flops | bytes accessed | tf_op | source)
XLA Modules:
  0.0 361.0 jit_solution(16243876525081524570)
XLA Ops:
  7.2 0.0 copy-start
  7.2 0.0 all-reduce.2.cloned.1.call-start
  7.2 40.3 %all-gather = bf16[32,4,3584]{2,1,0:T(4,128)(2,1)S(1)} all-gather(bf16[1,4,3584]{2,1,0:T(4,128)(2,1)} %bitcast.7), channel_id=1, replica_groups=mesh['section'=16,'tensor'=32] {'tensor'}, dimensions={0}, use_global_device_ids=true | all-gather | bytes 946176 | tf_op jit(solution)/shard_map/all_gather | solution.py:10
  47.5 0.0 copy-start.4
  47.5 0.2 reshape.22
  47.7 0.0 copy-start.1
  47.7 1.9 fusion.2
  49.7 0.0 copy-done
  49.7 0.0 copy-done.4
  49.7 1.2 fusion.7
  50.9 0.0 copy-done.1
  50.9 0.0 copy-start.3
  50.9 1.7 fusion.10
  52.6 0.0 all-reduce.2.cloned.1.call-update
  52.6 114.0 %psum.15 = f32[]{:T(128)} all-reduce(f32[]{:T(128)} %get-tuple-element.7), channel_id=1, replica_groups=mesh['section'=16,'tensor'=32] {'section','tensor'}, use_global_device_ids=true, to_apply=%region_6.0 | all-reduce | flops 1 | bytes 8 | tf_op jit(solution)/shard_map/psum | solution.py:19
  166.6 178.5 %all-reduce.2.cloned.1.call-done = f32[128,3584]{1,0:T(8,128)} async-done(((f32[128,3584]{1,0:T(8,128)}), f32[128,3584]{1,0:T(8,128)}) %all-reduce.2.cloned.1.call-update) | async-done | bytes 1835024 | tf_op jit(solution)/shard_map/psum | solution.py:24
  345.2 0.0 copy-done.3
  345.2 0.0 copy-start.2
  345.2 2.8 multiply_reduce_fusion
  348.0 0.0 copy-done.2
  348.0 1.3 convolution_add_fusion.1
  349.3 1.9 fusion
  351.2 0.6 constant_dynamic-slice_fusion
  (1 shorter events, 0.0 us)
Async XLA Ops:
  7.2 42.5 %copy-start = (bf16[224,3584]{1,0:T(8,128)(2,1)S(1)}, bf16[224,3584]{1,0:T(8,128)(2,1)}, u32[]{:S(2)}) copy-start(bf16[224,3584]{1,0:T(8,128)(2,1)} %param.6) | copy-start | bytes 4816900
  7.2 338.0 %all-reduce.2.cloned.1.call-start = ((), (), s32[]{:S(2)}) async-start(), calls=%async_computation | async-start | bytes 3670016 | tf_op jit(solution)/shard_map/psum | solution.py:24
  47.5 2.2 copy-start.4
  47.7 3.2 copy-start.1
  50.9 294.3 %copy-start.3 = (f32[3584]{0:T(1024)S(1)}, f32[3584]{0:T(1024)}, u32[]{:S(2)}) copy-start(f32[3584]{0:T(1024)} %param.9) | copy-start | bytes 43012
  345.2 2.8 copy-start.2
Sparse Core Ops, SparseCore 0:
  52.7 292.4 all-reduce.1
where the time goes:
time: 361 us
  waiting for transfers between devices  179 us (50%)
  blocking collectives  154 us (43%)
  between operations  16.4 us (5%)
  matrix products  6.08 us (2%)
  other arithmetic  4.75 us (1%)
    psum x1, waiting for transfers between devices, per_device(): summed = lax.psum(partial_value, ('section', 'tensor'))  179 us
    psum x1, blocking collectives, per_device(): penalty = lax.psum(jnp.sum(codes_f32 * dec_norm), ('section', 'tensor'))  114 us
    all_gather x1, blocking collectives, per_device(): stream = lax.all_gather(resid, 'tensor', axis=0, tiled=True)  40.3 us
  transfers between devices with their start and end apart: 1, of which 1 were waited for; matrix products, arithmetic and copies ran while one was open for 0% of the time, Pallas kernels for 0%

commit v1 on v0

--- a/solution.py
+++ b/solution.py
@@ -7,7 +7,9 @@
 
 
 def per_device(resid, w_enc, b_enc, w_dec, b_dec):
-    stream = lax.all_gather(resid, "tensor", axis=0, tiled=True)
+    stream = jnp.concatenate(
+        lax.all_to_all(jnp.stack([resid] * lax.axis_size("tensor")), "tensor", 0, 0), axis=0
+    )
     preact = (
         lax.dot_general(stream, w_enc, (((1,), (1,)), ((), ())), preferred_element_type=jnp.float32)
         + b_enc

time: 361 us -> 346 us (0.958)
  blocking collectives: 154 us -> 106 us
  waiting for transfers between devices: 179 us -> 199 us
  starting transfers between devices: 0.04 us -> 10.7 us
  local copies, waits for them, and re-layouts: 0.87 us -> 4.59 us
    all_gather x1 -> x0, blocking collectives: 40.3 us -> none  [per_device(): stream = lax.all_gather(resid, 'tensor', axis=0, tiled=True)]
    all_to_all x0 -> x1, waiting for transfers between devices: none -> 23 us  [per_device(): lax.all_to_all(jnp.stack([resid] * lax.axis_size('tensor')), 'tensor', 0, 0)]
    all_to_all x0 -> x1, starting transfers between devices: none -> 10.6 us  [per_device(): lax.all_to_all(jnp.stack([resid] * lax.axis_size('tensor')), 'tensor', 0, 0)]
    psum x1, blocking collectives: 114 us -> 106 us  [per_device(): penalty = lax.psum(jnp.sum(codes_f32 * dec_norm), ('section', 'tensor'))]
  transfers between devices with their start and end apart: 1 -> 2, of which waited for: 1 -> 2; matrix products, arithmetic and copies ran while one was open for 0% -> 0% of each run, Pallas kernels for 0% -> 0%
where the time goes in v1:
time: 346 us
  waiting for transfers between devices  199 us (58%)
  blocking collectives  106 us (31%)
  between operations  16.4 us (5%)
  starting transfers between devices  10.7 us (3%)
  matrix products  6.08 us (2%)
  local copies, waits for them, and re-layouts  4.59 us (1%)
    psum x1, waiting for transfers between devices, per_device(): summed = lax.psum(partial_value, ('section', 'tensor'))  176 us
    psum x1, blocking collectives, per_device(): penalty = lax.psum(jnp.sum(codes_f32 * dec_norm), ('section', 'tensor'))  106 us
    all_to_all x1, waiting for transfers between devices, per_device(): lax.all_to_all(jnp.stack([resid] * lax.axis_size('tensor')), 'tensor', 0, 0)  23 us
    all_to_all x1, starting transfers between devices, per_device(): lax.all_to_all(jnp.stack([resid] * lax.axis_size('tensor')), 'tensor', 0, 0)  10.6 us
  transfers between devices with their start and end apart: 2, of which 2 were waited for; matrix products, arithmetic and copies ran while one was open for 0% of the time, Pallas kernels for 0%

profile of v1, /device:TPU:1, one launch (start us, length us, event | category | flops | bytes accessed | tf_op | source)
XLA Modules:
  0.0 346.0 jit_solution(4959216329781461694)
XLA Ops:
  7.2 0.0 copy-start
  7.2 0.0 copy-start.1
  7.2 2.1 stack.2
  9.3 10.6 %all-to-all-start = ((bf16[32,4,3584]{2,1,0:T(4,128)(2,1)}), bf16[32,4,3584]{2,1,0:T(4,128)(2,1)}, u32[]{:S(2)}, u32[]{:S(2)}) async-start(bf16[32,4,3584]{2,1,0:T(4,128)(2,1)} %stack.2), calls=%async_computation | async-start | bytes 1835008 | tf_op jit(solution)/shard_map/all_to_all | solution.py:11
  19.9 0.0 copy-start.5
  19.9 0.0 all-reduce.2.cloned.1.call-start
  19.9 0.0 copy-done.1
  19.9 0.4 fusion.2
  20.4 23.0 %all-to-all-done = bf16[32,4,3584]{2,1,0:T(4,128)(2,1)} async-done(((bf16[32,4,3584]{2,1,0:T(4,128)(2,1)}), bf16[32,4,3584]{2,1,0:T(4,128)(2,1)}, u32[]{:S(2)}, u32[]{:S(2)}) %all-to-all-start) | async-done | bytes 917536 | tf_op jit(solution)/shard_map/all_to_all | solution.py:11
  43.3 1.7 reshape.26
  45.0 0.0 copy-done
  45.0 0.0 copy-done.5
  45.0 0.0 copy-start.2
  45.0 1.2 fusion.7
  46.2 0.2 copy-done.2
  46.4 0.0 copy-start.4
  46.4 1.7 fusion.10
  48.1 0.0 all-reduce.2.cloned.1.call-update
  48.1 106.0 %psum.15 = f32[]{:T(128)} all-reduce(f32[]{:T(128)} %get-tuple-element.7), channel_id=1, replica_groups=mesh['section'=16,'tensor'=32] {'section','tensor'}, use_global_device_ids=true, to_apply=%region_6.0 | all-reduce | flops 1 | bytes 8 | tf_op jit(solution)/shard_map/psum | solution.py:21
  154.1 176.1 %all-reduce.2.cloned.1.call-done = f32[128,3584]{1,0:T(8,128)} async-done(((f32[128,3584]{1,0:T(8,128)}), f32[128,3584]{1,0:T(8,128)}) %all-reduce.2.cloned.1.call-update) | async-done | bytes 1835024 | tf_op jit(solution)/shard_map/psum | solution.py:26
  330.2 0.0 copy-done.4
  330.2 0.0 copy-start.3
  330.2 2.8 multiply_reduce_fusion
  333.0 0.0 copy-done.3
  333.0 1.3 convolution_add_fusion.1
  334.3 1.9 fusion
  336.2 0.6 constant_dynamic-slice_fusion
  (1 shorter events, 0.0 us)
Async XLA Ops:
  7.2 37.8 %copy-start = (bf16[224,3584]{1,0:T(8,128)(2,1)S(1)}, bf16[224,3584]{1,0:T(8,128)(2,1)}, u32[]{:S(2)}) copy-start(bf16[224,3584]{1,0:T(8,128)(2,1)} %param.6) | copy-start | bytes 4816900
  7.2 12.8 %copy-start.1 = (bf16[224,3584]{1,0:T(8,128)(2,1)S(1)}, bf16[224,3584]{1,0:T(8,128)(2,1)}, u32[]{:S(2)}) copy-start(bf16[224,3584]{1,0:T(8,128)(2,1)} %param.8) | copy-start | bytes 4816900
  9.3 34.1 %all-to-all-start = ((bf16[32,4,3584]{2,1,0:T(4,128)(2,1)}), bf16[32,4,3584]{2,1,0:T(4,128)(2,1)}, u32[]{:S(2)}, u32[]{:S(2)}) async-start(bf16[32,4,3584]{2,1,0:T(4,128)(2,1)} %stack.2), calls=%async_computation | async-start | bytes 1835008 | tf_op jit(solution)/shard_map/all_to_all | solution.py:11
  19.9 25.1 %copy-start.5 = (f32[224]{0:T(256)S(1)}, f32[224]{0:T(256)}, u32[]{:S(2)}) copy-start(f32[224]{0:T(256)} %param.7) | copy-start | bytes 2692
  19.9 310.3 %all-reduce.2.cloned.1.call-start = ((), (), s32[]{:S(2)}) async-start(), calls=%async_computation.1 | async-start | bytes 3670016 | tf_op jit(solution)/shard_map/psum | solution.py:26
  45.0 1.4 copy-start.2
  46.4 283.8 %copy-start.4 = (f32[3584]{0:T(1024)S(1)}, f32[3584]{0:T(1024)}, u32[]{:S(2)}) copy-start(f32[3584]{0:T(1024)} %param.9) | copy-start | bytes 43012
  330.2 2.8 copy-start.3
Sparse Core Ops, SparseCore 0:
  48.2 281.8 all-reduce.1
